TPU v7x, 768 devices: a whole 4x8x12 slice. The times are simulated.
768 devices in a mesh: row: 16 (over z_hi, x, core), col: 48 (over y, z_lo).
Axes of the slice: x: 4, y: 8, z: 12 (z_hi: 2, z_lo: 6; z = z_hi * 6 + z_lo), core: 2. Of those that a mesh axis runs over, the one named last changes fastest.
Arguments:
- features: bfloat16 [48, 2048, 128], P('col', 'row'), may hold values from -6 to 6
- layer_weight: bfloat16 [128, 512], replicated, may hold values from -0.5 to 0.5
- cotangent: bfloat16 [16, 6144, 512], P('row', 'col'), may hold values from -6 to 6
- block_coords: int32 [16, 48, 32, 2], P('row', 'col'), may hold values from 0 to 47, as said below
- block_counts: int32 [16, 48], P('row', 'col'), may hold values from 1 to 32, as said below
- block_masks: int32 [16, 48, 32, 128, 128], P('row', 'col'), may hold values 0 or 1
- edge_weight: bfloat16 [16, 48, 32, 128, 128], P('row', 'col'), may hold values from 0.0099487305 to 0.06982422
Outputs:
- activated: bfloat16 [16, 6144, 512], P('row', 'col')
- feature_grad: bfloat16 [48, 2048, 128], P('col', 'row')
Inputs may be any that keep to these rules, and one draw needn't show every extreme that they name: `block_coords`: within one grid cell the first block_counts slots name distinct blocks; row entries lie in 0 to 47 and column entries in 0 to 15. `block_counts`: some grid cell uses all 32 slots.
All inputs are finite; a program needn't handle non-finite values. No bound on the sum of `block_masks` on one device may be relied on, other than what follows from the above.
Results may differ from a plain program's by a relative error of at most 0.0049.
Values may be sent and summed in bfloat16 or wider, within the bound.
A program may use at most 32 MiB of HBM per device.

v0:
```python
import jax
import jax.numpy as jnp
from jax import lax
from jax.sharding import PartitionSpec as P


def activation(value):
    return jax.nn.gelu(value, approximate=True)


def block_sums(prod, target, valid, out_blocks):
    block = prod.shape[1]
    width = prod.shape[2]
    onehot = (
        (target[:, None] == jnp.arange(out_blocks, dtype=jnp.int32)[None, :]) & valid[:, None]
    ).astype(jnp.float32)
    summed = jnp.einsum("kb,kif->bif", onehot, prod, precision=lax.Precision.HIGHEST)
    return summed.reshape(out_blocks * block, width)


def slot_products(blocks, source, panel):
    block = blocks.shape[-1]
    width = panel.shape[-1]
    taken = panel.reshape(-1, block, width)[source]
    return jnp.einsum("kij,kjf->kif", blocks, taken, preferred_element_type=jnp.float32)


def shards(features, layer_weight, cotangent, block_coords, block_counts, block_masks, edge_weight):
    highest = lax.Precision.HIGHEST
    block = block_masks.shape[-1]
    slab = cotangent.shape[1]
    rows_panel = slab * lax.axis_size("col") // block
    cols_panel = slab * lax.axis_size("row") // block
    slots = block_masks.shape[2]
    valid = jnp.arange(slots, dtype=jnp.int32) < block_counts[0, 0]
    blocks = block_masks[0, 0].astype(jnp.bfloat16) * edge_weight[0, 0]
    brow = block_coords[0, 0, :, 0]
    bcol = block_coords[0, 0, :, 1]
    weight_wide = layer_weight.astype(jnp.float32)
    panel = lax.all_gather(features, "row", axis=1, tiled=True)[0]
    prod = slot_products(blocks, bcol, panel)
    partial_value = block_sums(prod, brow, valid, rows_panel)
    aggregate = lax.psum_scatter(partial_value[None], "col", scatter_dimension=1, tiled=True)[0]
    pre = jnp.dot(aggregate, weight_wide, precision=highest)
    outputs, pullback = jax.vjp(activation, pre)
    gain = pullback(cotangent[0].astype(jnp.float32))[0]
    back = jnp.dot(gain, weight_wide.T, precision=highest).astype(jnp.bfloat16)
    back_panel = lax.all_gather(back[None], "col", axis=1, tiled=True)[0]
    transposed = jnp.swapaxes(blocks, 1, 2)
    prod_back = slot_products(transposed, brow, back_panel)
    partial_grad = block_sums(prod_back, bcol, valid, cols_panel)
    grad = lax.psum_scatter(partial_grad[None], "row", scatter_dimension=1, tiled=True)[0]
    return (outputs.astype(jnp.bfloat16)[None], grad.astype(jnp.bfloat16)[None])


def solution(mesh):
    return jax.shard_map(
        shards,
        mesh=mesh,
        in_specs=(
            P("col", "row", None),
            P(),
            P("row", "col", None),
            P("row", "col", None, None),
            P("row", "col"),
            P("row", "col", None, None, None),
            P("row", "col", None, None, None),
        ),
        out_specs=(P("row", "col", None), P("col", "row", None)),
        check_vma=False,
    )
```

profile of v0, /device:TPU:1, one launch (start us, length us, event | category | flops | bytes accessed | tf_op | source)
XLA Modules:
  0.0 784.5 jit_solution(5496014787022958707)
XLA Ops:
  7.2 0.0 copy-start
  7.2 0.0 copy-start.1
  7.2 0.0 reduce-scatter.3.cloned.1.call-start
  7.2 0.9 fusion.48
  8.1 0.8 slice_bitcast_fusion
  8.8 47.1 %all_gather.6 = bf16[1,2048,128]{2,1,0:T(8,128)(2,1)S(1)} all-gather(bf16[1,128,128]{2,1,0:T(8,128)(2,1)} %param.7), channel_id=1, replica_groups=mesh['row'=16,'col'=48] {'row'}, dimensions={1}, use_global_device_ids=true | all-gather | bytes 557056 | tf_op jit(solution)/shard_map/all_gather | solution.py:40
  56.6 1.6 gather_fusion
  58.2 0.0 copy-done.1
  58.3 2.0 fusion.6
  60.3 2.9 fusion.2
  63.2 2.6 copy.9
  65.8 0.0 copy-start.2
  65.8 0.0 reduce-scatter.3.cloned.1.call-update
  65.9 0.0 all-gather.3.cloned.1.call-start
  65.9 277.8 %reduce-scatter.3.cloned.1.call-done = f32[1,128,128]{2,1,0:T(8,128)} async-done(((f32[1,6144,128]{2,1,0:T(8,128)}), f32[1,128,128]{2,1,0:T(8,128)}) %reduce-scatter.3.cloned.1.call-update) | async-done | bytes 65552 | tf_op jit(solution)/shard_map/reduce_scatter | solution.py:43
  343.7 0.0 copy-done
  343.7 1.1 fusion.35
  344.8 0.0 copy-done.2
  344.8 1.1 convolution_convert_fusion
  345.9 0.0 all-gather.3.cloned.1.call-update
  345.9 0.0 reduce-scatter.5.cloned.1.call-start
  346.0 288.2 %all-gather.3.cloned.1.call-done = bf16[6144,128]{1,0:T(8,128)(2,1)} async-done(((bf16[128,128]{1,0:T(8,128)(2,1)}), bf16[6144,128]{1,0:T(8,128)(2,1)}) %all-gather.3.cloned.1.call-update) | async-done | bytes 1572880 | tf_op jit(solution)/shard_map/all_gather | solution.py:48
  634.2 2.2 gather_fusion.1
  636.4 1.8 fusion.4
  638.1 2.0 fusion
  640.1 1.3 copy.10
  641.4 0.0 reduce-scatter.5.cloned.1.call-update
  641.4 0.7 fusion.34
  642.2 134.3 %reduce-scatter.5.cloned.1.call-done = f32[1,128,128]{2,1,0:T(8,128)} async-done(((f32[1,2048,128]{2,1,0:T(8,128)}), f32[1,128,128]{2,1,0:T(8,128)}) %reduce-scatter.5.cloned.1.call-update) | async-done | bytes 65552 | tf_op jit(solution)/shard_map/reduce_scatter | solution.py:52
  776.5 1.5 convert_element_type.28
  (3 shorter events, 0.0 us)
Async XLA Ops:
  7.2 336.5 %copy-start = (bf16[128,512]{1,0:T(8,128)(2,1)S(1)}, bf16[128,512]{1,0:T(8,128)(2,1)}, u32[]{:S(2)}) copy-start(bf16[128,512]{1,0:T(8,128)(2,1)} %param.8) | copy-start | bytes 393220
  7.2 51.1 %copy-start.1 = (s32[1,1,32,128,128]{4,3,2,1,0:T(8,128)S(1)}, s32[1,1,32,128,128]{4,3,2,1,0:T(8,128)}, u32[]{:S(2)}) copy-start(s32[1,1,32,128,128]{4,3,2,1,0:T(8,128)} %param.12) | copy-start | bytes 6291460
  7.2 336.5 %reduce-scatter.3.cloned.1.call-start = ((), (), s32[]{:S(2)}) async-start(), calls=%async_computation.2 | async-start | bytes 3211264 | tf_op jit(solution)/shard_map/reduce_scatter | solution.py:43
  65.8 279.0 %copy-start.2 = (bf16[1,128,512]{2,1,0:T(8,128)(2,1)S(1)}, bf16[1,128,512]{2,1,0:T(8,128)(2,1)}, u32[]{:S(2)}) copy-start(bf16[1,128,512]{2,1,0:T(8,128)(2,1)} %param.9) | copy-start | bytes 393220
  65.9 568.3 %all-gather.3.cloned.1.call-start = ((), (), s32[]{:S(2)}) async-start(), calls=%async_computation.4 | async-start | bytes 1605632 | tf_op jit(solution)/shard_map/all_gather | solution.py:48
  345.9 430.6 %reduce-scatter.5.cloned.1.call-start = ((), (), s32[]{:S(2)}) async-start(), calls=%async_computation.3 | async-start | bytes 1114112 | tf_op jit(solution)/shard_map/reduce_scatter | solution.py:52
Sparse Core Ops, SparseCore 0:
  66.0 277.6 reduce-scatter.2
  346.9 287.2 all-gather.2
  641.6 134.9 reduce-scatter.4
where the time goes:
time: 785 us; the launch traced here: 784 us
  waiting for transfers between devices  700 us (89%)
  blocking collectives  47.1 us (6%)
  between operations  14.5 us (2%)
  matrix products  10.9 us (1%)
  local copies, waits for them, and re-layouts  8.47 us (1%)
    all_gather x1, waiting for transfers between devices, shards(): back_panel = lax.all_gather(back[None], 'col', axis=1, tiled=True)[0]  288 us
    reduce_scatter x1, waiting for transfers between devices, shards(): lax.psum_scatter(partial_value[None], 'col', scatter_dimension=1, tiled=T...  278 us
    reduce_scatter x1, waiting for transfers between devices, shards(): lax.psum_scatter(partial_grad[None], 'row', scatter_dimension=1, tiled=True)  134 us
    all_gather x1, blocking collectives, shards(): panel = lax.all_gather(features, 'row', axis=1, tiled=True)[0]  47.1 us
  transfers between devices with their start and end apart: 3, of which 3 were waited for; matrix products, arithmetic and copies ran while one was open for 0% of the time, Pallas kernels for 0%

commit v1 on v0

v1 whole, which is shorter than its diff:
```python
import functools

import jax
import jax.numpy as jnp
from jax import lax
from jax.experimental import pallas as pl
from jax.experimental.pallas import tpu as pltpu
from jax.sharding import PartitionSpec as P

MESH = pl.DeviceIdType.MESH
ZH, NX, NK = 2, 4, 2
NY, NZ = 8, 6
N_ROW, N_COL = ZH * NX * NK, NY * NZ
B = 128
H = B // 2
FI, FO = 128, 512
CAP = 32
HIGHEST = lax.Precision.HIGHEST
VMEM_LIMIT = 48 * 1024 * 1024


def row_coords():
    r = lax.axis_index("row")
    return r // (NX * NK), (r // NK) % NX, r % NK


def row_id(zh, x, k):
    return (zh * NX + x) * NK + k


def barrier(peers):
    sem = pltpu.get_barrier_semaphore()
    for peer in peers:
        pl.semaphore_signal(sem, inc=1, device_id=peer, device_id_type=MESH)
    pl.semaphore_wait(sem, len(peers))


def send(src, dst, send_sem, recv_sem, peer):
    copy = pltpu.make_async_remote_copy(
        src_ref=src, dst_ref=dst, send_sem=send_sem, recv_sem=recv_sem,
        device_id=peer, device_id_type=MESH,
    )
    copy.start()
    return copy


def gather_kernel(count_ref, feat_ref, mask_ref, weight_ref, panel_ref, blocks_ref, turned_ref,
                  mbuf, wbuf, load_sem, x_send, x_recv, z_send, z_recv, c_send, c_recv):
    zh, x, k = row_coords()
    c = lax.axis_index("col")
    here = row_id(zh, x, k)
    far = row_id(1 - zh, x, k)
    z_peer = (far, c)
    c_peer = (row_id(zh, x, 1 - k), c)
    x_to = [(x + d) % NX for d in (1, 2, 3)]
    x_from = [(x + NX - d) % NX for d in (1, 2, 3)]
    barrier([z_peer, c_peer] + [(row_id(zh, t, k), c) for t in x_to])
    sends = []
    panel_ref[here] = feat_ref[0]
    own = panel_ref.at[here]
    sends.append(send(own, own, z_send, z_recv, z_peer))
    for d in (0, 2, 1):
        sends.append(send(own, own, x_send.at[0, d], x_recv.at[0, d], (row_id(zh, x_to[d], k), c)))
    sends.append(send(own, own, c_send.at[0], c_recv.at[0], c_peer))
    loads = [
        pltpu.make_async_copy(mask_ref.at[0, 0], mbuf, load_sem.at[0]),
        pltpu.make_async_copy(weight_ref.at[0, 0], wbuf, load_sem.at[1]),
    ]
    for load in loads:
        load.start()
    for load in loads:
        load.wait()
    count = count_ref[0, 0]

    def build(slot, carry):
        keep = (mbuf[slot] * (slot < count).astype(jnp.int32)) != 0
        block = jnp.where(keep, wbuf[slot].astype(jnp.float32), 0.0)
        blocks_ref[slot] = block.astype(jnp.bfloat16)
        turned_ref[slot] = block.T.astype(jnp.bfloat16)
        return carry

    def arrived(block, sem):
        pltpu.make_async_copy(panel_ref.at[block], panel_ref.at[block], sem).wait()

    lax.fori_loop(0, CAP // 2, build, 0)
    for d in (0, 2, 1):
        block = row_id(zh, x_from[d], k)
        arrived(block, x_recv.at[0, d])
        ref = panel_ref.at[block]
        sends.append(send(ref, ref, c_send.at[1 + d], c_recv.at[1 + d], c_peer))
    lax.fori_loop(CAP // 2, CAP, build, 0)
    arrived(far, z_recv)
    ref = panel_ref.at[far]
    for d in (0, 2, 1):
        sends.append(send(ref, ref, x_send.at[1, d], x_recv.at[1, d], (row_id(zh, x_to[d], k), c)))
    sends.append(send(ref, ref, c_send.at[4], c_recv.at[4], c_peer))
    for d in (0, 2, 1):
        block = row_id(1 - zh, x_from[d], k)
        arrived(block, x_recv.at[1, d])
        ref = panel_ref.at[block]
        sends.append(send(ref, ref, c_send.at[5 + d], c_recv.at[5 + d], c_peer))
    for i, (h, t) in enumerate([(zh, x)] + [(zh, t) for t in x_from] + [(1 - zh, x)] + [(1 - zh, t) for t in x_from]):
        arrived(row_id(h, t, 1 - k), c_recv.at[i])
    for copy in sends:
        copy.wait_send()


def forward_kernel(coord_ref, blocks_ref, panel_ref, out_ref, prod):
    for slot in range(CAP):
        prod[slot] = jnp.dot(blocks_ref[slot], panel_ref[coord_ref[0, 0, slot, 1]], preferred_element_type=jnp.float32)
    out_ref[...] = jnp.zeros_like(out_ref)

    def add(slot, carry):
        b = coord_ref[0, 0, slot, 0]
        out_ref[b] = out_ref[b] + prod[slot]
        return carry

    lax.fori_loop(0, CAP, add, 0)


def backward_kernel(coord_ref, turned_ref, back_ref, out_ref, prod):
    for slot in range(CAP):
        prod[slot] = jnp.dot(turned_ref[slot], back_ref[coord_ref[0, 0, slot, 0]], preferred_element_type=jnp.float32)
    out_ref[...] = jnp.zeros_like(out_ref)

    def add(slot, carry):
        b = coord_ref[0, 0, slot, 1]
        at = (b % NK) * (ZH * NX) + b // NK
        out_ref[at] = out_ref[at] + prod[slot]
        return carry

    lax.fori_loop(0, CAP, add, 0)


def layer_kernel(part_ref, w_ref, cot_ref, act_ref, back_ref, r_out, l_out, r_in, l_in, z_out, z_in, total,
                 rs, rr, ls, lr, zs, zr, grs, grr, gls, glr, gzs, gzr):
    r = lax.axis_index("row")
    c = lax.axis_index("col")
    y, z = c // NZ, c % NZ
    right = (r, ((y + 1) % NY) * NZ + z)
    left = (r, ((y + NY - 1) % NY) * NZ + z)
    barrier([right, left] + [(r, y * NZ + (z + d) % NZ) for d in range(1, NZ)])

    def wait(ref, sem):
        pltpu.make_async_copy(ref, ref, sem).wait()

    low, high = pl.ds(0, H), pl.ds(H, H)

    def part(dy, j):
        return part_ref.at[((y + dy) % NY) * NZ + (z + 1 + j) % NZ]

    def first(j, carry):
        mine = part(4, j)
        r_out[0, j, :H] = mine[:H].astype(jnp.bfloat16)
        send(r_out.at[0, j, low], r_in.at[0, j, low], rs.at[0, j], rr.at[0, j], right)
        l_out[0, j, H:] = mine[H:].astype(jnp.bfloat16)
        send(l_out.at[0, j, high], l_in.at[0, j, high], ls.at[0, j], lr.at[0, j], left)
        return carry

    def second(j, carry):
        mine = part(3, j)
        r_out[1, j, H:] = mine[H:].astype(jnp.bfloat16)
        wait(r_in.at[0, j, low], rr.at[0, j])
        r_out[1, j, :H] = (mine[:H] + r_in[0, j, :H].astype(jnp.float32)).astype(jnp.bfloat16)
        send(r_out.at[1, j], r_in.at[1, j], rs.at[1, j], rr.at[1, j], right)
        mine = part(5, j)
        l_out[1, j, :H] = mine[:H].astype(jnp.bfloat16)
        wait(l_in.at[0, j, high], lr.at[0, j])
        l_out[1, j, H:] = (mine[H:] + l_in[0, j, H:].astype(jnp.float32)).astype(jnp.bfloat16)
        send(l_out.at[1, j], l_in.at[1, j], ls.at[1, j], lr.at[1, j], left)
        return carry

    def later(s, j, carry):
        wait(r_in.at[s - 1, j], rr.at[s - 1, j])
        r_out[s, j] = (part(4 - s, j)[...] + r_in[s - 1, j].astype(jnp.float32)).astype(jnp.bfloat16)
        send(r_out.at[s, j], r_in.at[s, j], rs.at[s, j], rr.at[s, j], right)
        wait(l_in.at[s - 1, j], lr.at[s - 1, j])
        l_out[s, j] = (part(4 + s, j)[...] + l_in[s - 1, j].astype(jnp.float32)).astype(jnp.bfloat16)
        send(l_out.at[s, j], l_in.at[s, j], ls.at[s, j], lr.at[s, j], left)
        return carry

    def collect(j):
        wait(r_in.at[3, j], rr.at[3, j])
        wait(l_in.at[3, j], lr.at[3, j])
        return part(0, j)[...] + r_in[3, j].astype(jnp.float32) + l_in[3, j].astype(jnp.float32)

    def pass_on(j, carry):
        z_out[j] = collect(j).astype(jnp.bfloat16)
        send(z_out.at[j], z_in.at[j], zs.at[j], zr.at[j], (r, y * NZ + (z + 1 + j) % NZ))
        return carry

    lax.fori_loop(0, NZ, first, 0)
    lax.fori_loop(0, NZ, second, 0)
    lax.fori_loop(0, NZ, functools.partial(later, 2), 0)
    lax.fori_loop(0, NZ, functools.partial(later, 3), 0)
    lax.fori_loop(0, NZ - 1, pass_on, 0)
    total[...] = collect(NZ - 1)

    def take(j, carry):
        wait(z_in.at[j], zr.at[j])
        total[...] = total[...] + z_in[j].astype(jnp.float32)
        return carry

    lax.fori_loop(0, NZ - 1, take, 0)

    weight = w_ref[...].astype(jnp.float32)
    pre = jnp.dot(total[...], weight, precision=HIGHEST, preferred_element_type=jnp.float32)
    scale = 0.7978845608028654
    t = jnp.tanh(scale * (pre + 0.044715 * (pre * pre * pre)))
    cdf = 0.5 * (1.0 + t)
    act_ref[0] = (pre * cdf).astype(jnp.bfloat16)
    slope = cdf + pre * (0.5 * (1.0 - t * t)) * (scale * (1.0 + 3 * 0.044715 * (pre * pre)))
    gain = cot_ref[0].astype(jnp.float32) * slope
    back = lax.dot_general(gain, weight, (((1,), (1,)), ((), ())), precision=HIGHEST,
                           preferred_element_type=jnp.float32)
    back_ref[c] = back.astype(jnp.bfloat16)

    def block(dy, j):
        return back_ref.at[((y + dy) % NY) * NZ + (z + j) % NZ]

    def hop(s, j):
        if s < 3:
            ref = block(NY - s, j)
            send(ref, ref, grs.at[s, j], grr.at[s, j], right)
            ref = block(s, j)
            send(ref, ref, gls.at[s, j], glr.at[s, j], left)
        else:
            ref = block(NY - 3, j).at[low]
            send(ref, ref, grs.at[s, j], grr.at[s, j], right)
            ref = block(3, j).at[high]
            send(ref, ref, gls.at[s, j], glr.at[s, j], left)

    own = block(0, 0)
    hop(0, 0)
    for d in (1, 5, 2, 4, 3):
        send(own, own, gzs.at[d], gzr.at[d], (r, y * NZ + (z + d) % NZ))
    for d in (5, 1, 4, 2, 3):
        j = NZ - d
        wait(block(0, j), gzr.at[d])
        hop(0, j)

    def onward(s, j, carry):
        wait(block(NY - s, j), grr.at[s - 1, j])
        wait(block(s, j), glr.at[s - 1, j])
        hop(s, j)
        return carry

    for s in (1, 2, 3):
        lax.fori_loop(0, NZ, functools.partial(onward, s), 0)

    def finish(j, carry):
        wait(block(4, j).at[low], grr.at[3, j])
        wait(block(4, j).at[high], glr.at[3, j])
        return carry

    lax.fori_loop(0, NZ, finish, 0)

    def drain(j, carry):
        half = r_out.at[0, j, low]
        full = r_out.at[1, j]
        for s in range(4):
            wait(half if s == 0 else full, rs.at[s, j])
            wait(half if s == 0 else full, ls.at[s, j])
            wait(half if s == 3 else full, grs.at[s, j])
            wait(half if s == 3 else full, gls.at[s, j])
        return carry

    lax.fori_loop(0, NZ, drain, 0)
    for j in range(NZ - 1):
        wait(z_out.at[j], zs.at[j])
        wait(z_out.at[j], gzs.at[j + 1])


def scatter_kernel(part_ref, out_ref, c_in, x_out, x_in, z_out, z_in, cs, cr, xs, xr, zs, zr):
    zh, x, k = row_coords()
    c = lax.axis_index("col")
    z_peer = (row_id(1 - zh, x, k), c)
    c_peer = (row_id(zh, x, 1 - k), c)
    x_to = [(x + d) % NX for d in (1, 2, 3)]
    x_peers = [(row_id(zh, t, k), c) for t in x_to]
    barrier([z_peer, c_peer] + x_peers)
    halves = (1 - zh, zh)
    sends = []
    for i, h in enumerate(halves):
        at = pl.ds(h * NX, NX)
        sends.append(send(part_ref.at[1 - k, at], c_in.at[at], cs.at[i], cr.at[i], c_peer))
    total = None
    for i, h in enumerate(halves):
        at = c_in.at[pl.ds(h * NX, NX)]
        pltpu.make_async_copy(at, at, cr.at[i]).wait()
        for d in (1, 0, 2):
            b = h * NX + x_to[d]
            x_out[i, d] = (part_ref[k, b] + c_in[b]).astype(jnp.bfloat16)
            sends.append(send(x_out.at[i, d], x_in.at[i, d], xs.at[i, d], xr.at[i, d], x_peers[d]))
    for i, h in enumerate(halves):
        b = h * NX + x
        total = part_ref[k, b] + c_in[b]
        for d in (0, 2, 1):
            pltpu.make_async_copy(x_in.at[i, d], x_in.at[i, d], xr.at[i, d]).wait()
            total = total + x_in[i, d].astype(jnp.float32)
        if i == 0:
            z_out[...] = total.astype(jnp.bfloat16)
            sends.append(send(z_out, z_in, zs, zr, z_peer))
    pltpu.make_async_copy(z_in, z_in, zr).wait()
    out_ref[0] = (total + z_in[...].astype(jnp.float32)).astype(jnp.bfloat16)
    for copy in sends:
        copy.wait_send()


def shards(features, layer_weight, cotangent, block_coords, block_counts, block_masks, edge_weight):
    vmem = pl.BlockSpec(memory_space=pltpu.VMEM)
    smem = pl.BlockSpec(memory_space=pltpu.SMEM)
    hbm = pl.BlockSpec(memory_space=pl.ANY)
    dma = pltpu.SemaphoreType.DMA
    bf16, f32 = jnp.bfloat16, jnp.float32

    def params(**kw):
        return pltpu.CompilerParams(vmem_limit_bytes=VMEM_LIMIT, **kw)

    panel, blocks, turned = pl.pallas_call(
        gather_kernel,
        out_shape=(
            jax.ShapeDtypeStruct((N_ROW, B, FI), bf16),
            jax.ShapeDtypeStruct((CAP, B, B), bf16),
            jax.ShapeDtypeStruct((CAP, B, B), bf16),
        ),
        in_specs=[smem, vmem, hbm, hbm],
        out_specs=(vmem, vmem, vmem),
        scratch_shapes=[
            pltpu.VMEM((CAP, B, B), jnp.int32), pltpu.VMEM((CAP, B, B), bf16), dma((2,)),
            dma((2, 3)), dma((2, 3)), dma, dma, dma((8,)), dma((8,)),
        ],
        compiler_params=params(collective_id=0, has_side_effects=True),
    )(block_counts, features, block_masks, edge_weight)

    partial_value = pl.pallas_call(
        forward_kernel,
        out_shape=jax.ShapeDtypeStruct((N_COL, B, FI), f32),
        in_specs=[smem, vmem, vmem],
        out_specs=vmem,
        scratch_shapes=[pltpu.VMEM((CAP, B, FI), f32)],
        compiler_params=params(),
    )(block_coords, blocks, panel)

    activated, back = pl.pallas_call(
        layer_kernel,
        out_shape=(jax.ShapeDtypeStruct((1, B, FO), bf16), jax.ShapeDtypeStruct((N_COL, B, FI), bf16)),
        in_specs=[vmem, vmem, vmem],
        out_specs=(vmem, vmem),
        scratch_shapes=[pltpu.VMEM((4, NZ, B, FI), bf16)] * 4
        + [pltpu.VMEM((NZ, B, FI), bf16)] * 2
        + [pltpu.VMEM((B, FI), f32)]
        + [dma((4, NZ))] * 4 + [dma((NZ,))] * 2 + [dma((4, NZ))] * 4 + [dma((NZ,))] * 2,
        compiler_params=params(collective_id=1, has_side_effects=True),
    )(partial_value, layer_weight, cotangent)

    partial_grad = pl.pallas_call(
        backward_kernel,
        out_shape=jax.ShapeDtypeStruct((N_ROW, B, FI), f32),
        in_specs=[smem, vmem, vmem],
        out_specs=vmem,
        scratch_shapes=[pltpu.VMEM((CAP, B, FI), f32)],
        compiler_params=params(),
    )(block_coords, turned, back)

    grad = pl.pallas_call(
        scatter_kernel,
        out_shape=jax.ShapeDtypeStruct((1, B, FI), bf16),
        in_specs=[vmem],
        out_specs=vmem,
        scratch_shapes=[
            pltpu.VMEM((ZH * NX, B, FI), f32),
            pltpu.VMEM((2, 3, B, FI), bf16), pltpu.VMEM((2, 3, B, FI), bf16),
            pltpu.VMEM((B, FI), bf16), pltpu.VMEM((B, FI), bf16),
            dma((2,)), dma((2,)), dma((2, 3)), dma((2, 3)), dma, dma,
        ],
        compiler_params=params(collective_id=2, has_side_effects=True),
    )(partial_grad.reshape(NK, ZH * NX, B, FI))
    return activated, grad


def solution(mesh):
    return jax.shard_map(
        shards,
        mesh=mesh,
        in_specs=(
            P("col", "row", None),
            P(),
            P("row", "col", None),
            P("row", "col", None, None),
            P("row", "col"),
            P("row", "col", None, None, None),
            P("row", "col", None, None, None),
        ),
        out_specs=(P("row", "col", None), P("col", "row", None)),
        check_vma=False,
    )
```

time: 785 us -> 111 us (0.14)
  waiting for transfers between devices: 700 us -> 0 us
  Pallas kernels: 0 us -> 104 us
  blocking collectives: 47.1 us -> 0 us
  between operations: 14.5 us -> 1.35 us
  matrix products: 10.9 us -> 0 us
    reduce_scatter x2 -> x0, waiting for transfers between devices: 412 us -> none  [the longest x1 278 us: shards(): lax.psum_scatter(partial_value[None], 'col', scatter_dimension=1, tiled=T...]
    all_gather x1 -> x0, waiting for transfers between devices: 288 us -> none  [shards(): back_panel = lax.all_gather(back[None], 'col', axis=1, tiled=True)[0]]
    pallas_call x0 -> x5, Pallas kernels: none -> 104 us  [the longest x1 50.1 us: shards(): pl.pallas_call(layer_kernel, out_shape=(jax.ShapeDtypeStruct((1, B, FO),...]
    all_gather x1 -> x0, blocking collectives: 47.1 us -> none  [shards(): panel = lax.all_gather(features, 'row', axis=1, tiled=True)[0]]
    dot_general x6 -> x0, matrix products: 10.9 us -> none  [the longest x2 4.95 us: block_sums(): jnp.einsum('kb,kif->bif', onehot, prod, precision=lax.Precision.HIGHEST)]
  transfers between devices with their start and end apart: 3 -> 0, of which waited for: 3 -> 0; matrix products, arithmetic and copies ran while one was open for 0% -> 0% of each run, Pallas kernels for 0% -> 0%
where the time goes in v1:
time: 111 us
  Pallas kernels  104 us (94%)
  local copies, waits for them, and re-layouts  5.62 us (5%)
  between operations  1.35 us (1%)
    pallas_call x1, Pallas kernels, shards(): pl.pallas_call(layer_kernel, out_shape=(jax.ShapeDtypeStruct((1, B, FO),...  50.1 us
    pallas_call x1, Pallas kernels, shards(): pl.pallas_call(gather_kernel, out_shape=(jax.ShapeDtypeStruct((N_ROW, B,...  26.9 us
    pallas_call x1, Pallas kernels, shards(): pl.pallas_call(scatter_kernel, out_shape=jax.ShapeDtypeStruct((1, B, FI),...  23.3 us
    unnamed x13, local copies, waits for them, and re-layouts  5.62 us

profile of v1, /device:TPU:1, one launch (start us, length us, event | category | flops | bytes accessed | tf_op | source)
XLA Modules:
  0.0 110.9 jit_solution(11013587653303254557)
XLA Ops:
  1.3 0.8 copy.9.coord_ref
  2.0 0.0 copy-start
  2.0 1.6 %copy-done = s32[1,1,32,128,128]{4,3,2,1,0:T(8,128)S(1)} copy-done((s32[1,1,32,128,128]{4,3,2,1,0:T(8,128)S(1)}, s32[1,1,32,128,128]{4,3,2,1,0:T(8,128)}, u32[]{:S(2)}) %copy-start) | copy-done | bytes 2097176
  3.6 0.0 copy-start.1
  3.6 1.2 %copy-done.1 = bf16[1,1,32,128,128]{4,3,2,1,0:T(8,128)(2,1)S(1)} copy-done((bf16[1,1,32,128,128]{4,3,2,1,0:T(8,128)(2,1)S(1)}, bf16[1,1,32,128,128]{4,3,2,1,0:T(8,128)(2,1)}, u32[]{:S(2)}) %copy-start.1) | copy-done | bytes 1048600
  4.9 0.0 copy-start.4
  4.9 0.8 copy-done.4
  5.6 26.9 %shard_map.86 = (bf16[16,128,128]{2,1,0:T(8,128)(2,1)S(1)}, bf16[32,128,128]{2,1,0:T(8,128)(2,1)S(1)}, bf16[32,128,128]{2,1,0:T(8,128)(2,1)S(1)}) custom-call(s32[1,1]{1,0:T(1,128)S(6)} %copy.13.count_ref, bf16[1,128,128]{2,1,0:T(8,128)(2,1)S(1)} %copy-done.4, s32[1,1,32,128,128]{4,3,2,1,0:T(8,128)S(1)} %copy-done, bf16[1,1,32,128,128]{4,3,2,1,0:T(8,128)(2,1)S(1)} %copy-done.1), custom_call_target="tpu_custom_call" | custom-call | tf_op jit(solution)/shard_map/pallas_call | solution.py:320
  32.5 0.0 copy-start.2
  32.5 0.0 copy-start.3
  32.5 1.8 %shard_map.87.part_ref = f32[48,128,128]{2,1,0:T(8,128)S(1)} custom-call(s32[1,1,32,2]{3,2,1,0:T(8,128)S(1)} %copy.9.coord_ref, bf16[32,128,128]{2,1,0:T(8,128)(2,1)S(1)} %get-tuple-element.7.blocks_ref, bf16[16,128,128]{2,1,0:T(8,128)(2,1)S(1)} %get-tuple-element.8.panel_ref), custom_call_target="tpu_custom_call" | custom-call | tf_op jit(solution)/shard_map/pallas_call | solution.py:336
  34.3 0.0 copy-done.2
  34.3 0.0 copy-done.3
  34.3 50.1 %shard_map.88 = (bf16[1,128,512]{2,1,0:T(8,128)(2,1)S(1)}, bf16[48,128,128]{2,1,0:T(8,128)(2,1)S(1)}) custom-call(f32[48,128,128]{2,1,0:T(8,128)S(1)} %shard_map.87.part_ref, bf16[128,512]{1,0:T(8,128)(2,1)S(1)} %copy-done.2, bf16[1,128,512]{2,1,0:T(8,128)(2,1)S(1)} %copy-done.3), custom_call_target="tpu_custom_call" | custom-call | tf_op jit(solution)/shard_map/pallas_call | solution.py:345
  84.5 1.8 %shard_map.89 = f32[16,128,128]{2,1,0:T(8,128)S(1)} custom-call(s32[1,1,32,2]{3,2,1,0:T(8,128)S(1)} %copy.9.coord_ref, bf16[32,128,128]{2,1,0:T(8,128)(2,1)S(1)} %get-tuple-element.10.turned_ref, bf16[48,128,128]{2,1,0:T(8,128)(2,1)S(1)} %get-tuple-element.11.back_ref), custom_call_target="tpu_custom_call" | custom-call | tf_op jit(solution)/shard_map/pallas_call | solution.py:357
  86.3 23.3 %shard_map.90 = bf16[1,128,128]{2,1,0:T(8,128)(2,1)S(1)} custom-call(f32[2,8,128,128]{3,2,1,0:T(8,128)S(1)} %bitcast.1), custom_call_target="tpu_custom_call" | custom-call | tf_op jit(solution)/shard_map/pallas_call | solution.py:366
  109.6 0.7 copy.14
  110.3 0.6 copy.15
Async XLA Ops:
  2.0 1.6 %copy-start = (s32[1,1,32,128,128]{4,3,2,1,0:T(8,128)S(1)}, s32[1,1,32,128,128]{4,3,2,1,0:T(8,128)}, u32[]{:S(2)}) copy-start(s32[1,1,32,128,128]{4,3,2,1,0:T(8,128)} %mask_ref.1) | copy-start | bytes 6291460
  3.6 1.2 %copy-start.1 = (bf16[1,1,32,128,128]{4,3,2,1,0:T(8,128)(2,1)S(1)}, bf16[1,1,32,128,128]{4,3,2,1,0:T(8,128)(2,1)}, u32[]{:S(2)}) copy-start(bf16[1,1,32,128,128]{4,3,2,1,0:T(8,128)(2,1)} %weight_ref.1) | copy-start | bytes 3145732
  4.9 0.8 copy-start.4
  32.5 1.8 %copy-start.2 = (bf16[128,512]{1,0:T(8,128)(2,1)S(1)}, bf16[128,512]{1,0:T(8,128)(2,1)}, u32[]{:S(2)}) copy-start(bf16[128,512]{1,0:T(8,128)(2,1)} %w_ref.1) | copy-start | bytes 393220
  32.5 1.8 %copy-start.3 = (bf16[1,128,512]{2,1,0:T(8,128)(2,1)S(1)}, bf16[1,128,512]{2,1,0:T(8,128)(2,1)}, u32[]{:S(2)}) copy-start(bf16[1,128,512]{2,1,0:T(8,128)(2,1)} %cot_ref.1) | copy-start | bytes 393220

commit v2 on v0

v2 whole, which is shorter than its diff:
```python
import jax
import jax.numpy as jnp
from jax import lax
from jax.experimental import pallas as pl
from jax.experimental.pallas import tpu as pltpu
from jax.sharding import PartitionSpec as P

MESH = pl.DeviceIdType.MESH
ZH, NX, NK = 2, 4, 2
NY, NZ = 8, 6
N_ROW, N_COL = ZH * NX * NK, NY * NZ
B = 128
H = B // 2
FI, FO = 128, 512
CAP = 32
STEPS = 4
HALF = STEPS * NZ - NZ // 2
HIGHEST = lax.Precision.HIGHEST
VMEM_LIMIT = 60 * 1024 * 1024
f32, bf16, i32 = jnp.float32, jnp.bfloat16, jnp.int32


def row_id(zh, x, k):
    return (zh * NX + x) * NK + k


def send(src, dst, send_sem, recv_sem, peer):
    pltpu.make_async_remote_copy(
        src_ref=src, dst_ref=dst, send_sem=send_sem, recv_sem=recv_sem,
        device_id=peer, device_id_type=MESH,
    ).start()


def wait(ref, sem):
    pltpu.make_async_copy(ref, ref, sem).wait()


def near(z, i):
    m = jnp.minimum(z, NZ - 1 - z)
    v = jnp.where(i > 2 * m, i, jnp.where(i % 2 == 1, m - (i + 1) // 2, m + i // 2))
    return jnp.where(z < NZ // 2, v, NZ - 1 - v)


def sort_tables(key, other):
    k_sub = lax.broadcasted_iota(i32, (CAP, CAP), 0)
    k_lane = lax.broadcasted_iota(i32, (CAP, CAP), 1)
    eye = k_sub == k_lane

    def upright(v):
        return jnp.sum(jnp.where(eye, jnp.broadcast_to(v, (CAP, CAP)), 0), axis=1, keepdims=True)

    key_c = upright(key)
    before = (key_c < key) | ((key_c == key) & (k_sub < k_lane))
    rank = jnp.sum(before.astype(i32), axis=0, keepdims=True)
    lanes = lax.broadcasted_iota(i32, (CAP, 128), 1)
    at = upright(rank) == lanes

    def place(col):
        return jnp.sum(jnp.where(at, col, 0), axis=0, keepdims=True)

    order = place(lax.broadcasted_iota(i32, (CAP, 128), 0))
    source = place(jnp.broadcast_to(upright(other), (CAP, 128)))
    sorted_key = place(jnp.broadcast_to(key_c, (CAP, 128)))
    start = jnp.sum((key_c < sorted_key).astype(i32), axis=0, keepdims=True)
    same = (start != lanes[:1]).astype(i32)
    below = jnp.sum((key_c < lanes).astype(i32), axis=0, keepdims=True)
    upto = jnp.sum((key_c <= lanes).astype(i32), axis=0, keepdims=True)
    last = jnp.where(upto > below, upto, 0)
    return [order, source, same, last]


def kernel(count_ref, coord_hbm, feat_hbm, w_hbm, cot_hbm, mask_hbm, weight_hbm, act_ref, grad_ref,
           panel, coord, mbuf, wbuf, blocks, wide, cot, table, tab, sums,
           r_out, l_out, r_in, l_in, z_out, z_in, back,
           stage, c_in, x_out, x_in, q_out, q_in,
           load, fs, fx, fz, fc, rs, rr, ls, lr, zs, zr, grs, grr, gls, glr, gzs, gzr, es, ec, exs, ex, ezs, ez):
    r = lax.axis_index("row")
    c = lax.axis_index("col")
    zh, x, k = r // (NX * NK), (r // NK) % NX, r % NK
    y, z = c // NZ, c % NZ
    far = row_id(1 - zh, x, k)
    z_peer = (far, c)
    c_peer = (row_id(zh, x, 1 - k), c)
    x_to = [(x + d) % NX for d in (1, 2, 3)]
    x_from = [(x + NX - d) % NX for d in (1, 2, 3)]
    x_peers = [(row_id(zh, t, k), c) for t in x_to]
    right = (r, ((y + 1) % NY) * NZ + z)
    left = (r, ((y + NY - 1) % NY) * NZ + z)
    peers = [z_peer] + x_peers + [right, left] + [(r, y * NZ + (z + d) % NZ) for d in range(1, NZ)] + [c_peer]
    gate = pltpu.get_barrier_semaphore()
    for peer in peers:
        pl.semaphore_signal(gate, inc=1, device_id=peer, device_id_type=MESH)
    local = [
        pltpu.make_async_copy(feat_hbm.at[0], panel.at[r], load.at[0]),
        pltpu.make_async_copy(coord_hbm.at[0, 0], coord, load.at[1]),
        pltpu.make_async_copy(mask_hbm.at[0, 0], mbuf, load.at[2]),
        pltpu.make_async_copy(weight_hbm.at[0, 0], wbuf, load.at[3]),
        pltpu.make_async_copy(w_hbm, wide, load.at[4]),
        pltpu.make_async_copy(cot_hbm.at[0], cot, load.at[5]),
    ]
    for copy in local:
        copy.start()
    local[0].wait()
    pl.semaphore_wait(gate, len(peers))

    own = panel.at[r]
    send(own, own, fs, fz, z_peer)
    for d in (0, 2, 1):
        send(own, own, fs, fx.at[0, d], x_peers[d])
    send(own, own, fs, fc.at[0], c_peer)

    local[1].wait()
    valid = lax.broadcasted_iota(i32, (1, CAP), 1) < count_ref[0, 0]
    brow = jnp.where(valid, coord[0:1, :], 0)
    bcol = jnp.where(valid, coord[1:2, :], 0)
    rows = sort_tables(jnp.where(valid, brow, N_COL), bcol) + sort_tables(jnp.where(valid, bcol, N_COL), brow)
    table[...] = jnp.concatenate(rows, axis=0)
    lookup = pltpu.make_async_copy(table, tab, load.at[1])
    lookup.start()
    local[2].wait()
    local[3].wait()

    def build(slot, carry):
        blocks[slot] = jnp.where(mbuf[slot] != 0, wbuf[slot].astype(f32), 0.0).astype(bf16)
        return carry

    lax.fori_loop(0, CAP // 2, build, 0)
    for d in (0, 2, 1):
        ref = panel.at[row_id(zh, x_from[d], k)]
        wait(ref, fx.at[0, d])
        send(ref, ref, fs, fc.at[1 + d], c_peer)
    lax.fori_loop(CAP // 2, CAP, build, 0)
    lookup.wait()
    sums[0] = jnp.zeros((B, FI), f32)

    ref = panel.at[far]
    wait(ref, fz)
    for d in (0, 2, 1):
        send(ref, ref, fs, fx.at[1, d], x_peers[d])
    send(ref, ref, fs, fc.at[4], c_peer)
    for d in (0, 2, 1):
        ref = panel.at[row_id(1 - zh, x_from[d], k)]
        wait(ref, fx.at[1, d])
        send(ref, ref, fs, fc.at[5 + d], c_peer)
    for i, (h, t) in enumerate([(zh, x)] + [(zh, t) for t in x_from] + [(1 - zh, x)] + [(1 - zh, t) for t in x_from]):
        wait(panel.at[row_id(h, t, 1 - k)], fc.at[i])

    def scan(at, product):
        def eight(g, run):
            for i in range(8):
                p = g * 8 + i
                new = product(tab[at, p], tab[at + 1, p])
                run = run * tab[at + 2, p].astype(f32) + new
                sums[p + 1] = run
            return run

        lax.fori_loop(0, CAP // 8, eight, jnp.zeros((B, FI), f32))

    scan(0, lambda slot, source: jnp.dot(blocks[slot], panel[source], preferred_element_type=f32))

    low, high = pl.ds(0, H), pl.ds(H, H)

    def dest(j):
        return near(z, NZ - 1 - j)

    def part(dy, j):
        return sums[tab[3, ((y + dy) % NY) * NZ + dest(j)]]

    def first(j, carry):
        mine = part(4, j).astype(bf16)
        r_out[j, :H] = mine[:H]
        send(r_out.at[j, low], r_in.at[j, low], rs, rr.at[j], right)
        l_out[j, H:] = mine[H:]
        send(l_out.at[j, high], l_in.at[j, high], ls, lr.at[j], left)
        return carry

    def second(j, carry):
        t = NZ + j
        mine = part(3, j)
        wait(r_in.at[j, low], rr.at[j])
        r_out[t, H:] = mine[H:].astype(bf16)
        r_out[t, :H] = (mine[:H] + r_in[j, :H].astype(f32)).astype(bf16)
        send(r_out.at[t], r_in.at[t], rs, rr.at[t], right)
        mine = part(5, j)
        wait(l_in.at[j, high], lr.at[j])
        l_out[t, :H] = mine[:H].astype(bf16)
        l_out[t, H:] = (mine[H:] + l_in[j, H:].astype(f32)).astype(bf16)
        send(l_out.at[t], l_in.at[t], ls, lr.at[t], left)
        return carry

    def later(i, carry):
        s, j = 2 + i // NZ, i % NZ
        t = s * NZ + j
        wait(r_in.at[t - NZ], rr.at[t - NZ])
        r_out[t] = (part(STEPS - s, j) + r_in[t - NZ].astype(f32)).astype(bf16)
        send(r_out.at[t], r_in.at[t], rs, rr.at[t], right)
        wait(l_in.at[t - NZ], lr.at[t - NZ])
        l_out[t] = (part(STEPS + s, j) + l_in[t - NZ].astype(f32)).astype(bf16)
        send(l_out.at[t], l_in.at[t], ls, lr.at[t], left)
        return carry

    def collect(j):
        t = 3 * NZ + j
        wait(r_in.at[t], rr.at[t])
        wait(l_in.at[t], lr.at[t])
        return part(0, j) + r_in[t].astype(f32) + l_in[t].astype(f32)

    def pass_on(j, carry):
        z_out[j] = collect(j).astype(bf16)
        send(z_out.at[j], z_in.at[z], zs, zr.at[z], (r, y * NZ + dest(j)))
        return carry

    lax.fori_loop(0, NZ, first, 0)
    lax.fori_loop(0, NZ, second, 0)
    lax.fori_loop(0, 2 * NZ, later, 0)
    lax.fori_loop(0, NZ - 1, pass_on, 0)

    wait(panel.at[pl.ds(0, 15)], fs)
    wait(r_out.at[pl.ds(0, HALF)], rs)
    wait(l_out.at[pl.ds(0, HALF)], ls)
    local[4].wait()
    local[5].wait()
    weight = wide[...].astype(f32)

    def take(i, run):
        other = near(z, i)
        wait(z_in.at[other], zr.at[other])
        return run + z_in[other].astype(f32)

    total = lax.fori_loop(1, NZ, take, collect(NZ - 1))

    pre = jnp.dot(total, weight, precision=HIGHEST, preferred_element_type=f32)
    scale = 0.7978845608028654
    t = jnp.tanh(scale * (pre + 0.044715 * (pre * pre * pre)))
    cdf = 0.5 * (1.0 + t)
    slope = cdf + pre * (0.5 * (1.0 - t * t)) * (scale * (1.0 + 3 * 0.044715 * (pre * pre)))
    gain = cot[...].astype(f32) * slope
    turned = lax.dot_general(weight, gain, (((1,), (1,)), ((), ())), precision=HIGHEST, preferred_element_type=f32)
    back[c] = turned.astype(bf16)

    def block(dy, j):
        return back.at[((y + dy) % NY) * NZ + near(z, j)]

    def hop(s, j):
        t = s * NZ + j
        if s < STEPS - 1:
            right_ref, left_ref = block(NY - s, j), block(s, j)
        else:
            right_ref, left_ref = block(NY - s, j).at[low], block(s, j).at[high]
        send(right_ref, right_ref, grs, grr.at[t], right)
        send(left_ref, left_ref, gls, glr.at[t], left)

    mine = back.at[c]
    for j in range(1, NZ):
        send(mine, mine, gzs, gzr.at[z], (r, y * NZ + near(z, NZ - j)))
    act_ref[0] = (pre * cdf).astype(bf16)

    def wave(i, carry):
        for s in range(STEPS - 1, 0, -1):
            j = i - 3 * s

            @pl.when((j >= 0) & (j < NZ))
            def _():
                t = (s - 1) * NZ + j
                wait(block(NY - s, j), grr.at[t])
                wait(block(s, j), glr.at[t])
                hop(s, j)

        @pl.when((i > 0) & (i < NZ))
        def _():
            other = near(z, i)
            wait(back.at[y * NZ + other], gzr.at[other])

        @pl.when(i < NZ)
        def _():
            hop(0, i)

        return carry

    lax.fori_loop(0, NZ + 3 * (STEPS - 1), wave, 0)
    wait(z_out, zs)

    def finish(j, carry):
        t = (STEPS - 1) * NZ + j
        wait(block(STEPS, j).at[low], grr.at[t])
        wait(block(STEPS, j).at[high], glr.at[t])
        return carry

    lax.fori_loop(0, NZ, finish, 0)

    scan(4, lambda slot, source: jnp.dot(back[source], blocks[slot], preferred_element_type=f32))

    def grad(h, t, core):
        return sums[tab[7, row_id(h, t, core)]]

    halves = (1 - zh, zh)
    for i, h in enumerate(halves):
        for t in range(NX):
            stage[h * NX + t] = grad(h, t, 1 - k)
        at = pl.ds(h * NX, NX)
        send(stage.at[at], c_in.at[at], es, ec.at[i], c_peer)
    for i, h in enumerate(halves):
        wait(c_in.at[pl.ds(h * NX, NX)], ec.at[i])
        for d in (1, 0, 2):
            x_out[i * 3 + d] = (grad(h, x_to[d], k) + c_in[h * NX + x_to[d]]).astype(bf16)
            send(x_out.at[i * 3 + d], x_in.at[i * 3 + d], exs, ex.at[i * 3 + d], x_peers[d])
    for i, h in enumerate(halves):
        run = grad(h, x, k) + c_in[h * NX + x]
        for d in (0, 2, 1):
            wait(x_in.at[i * 3 + d], ex.at[i * 3 + d])
            run = run + x_in[i * 3 + d].astype(f32)
        if i == 0:
            q_out[...] = run.astype(bf16)
            send(q_out, q_in, ezs, ez, z_peer)
    wait(back.at[pl.ds(0, HALF)], grs)
    wait(back.at[pl.ds(0, HALF)], gls)
    wait(z_out, gzs)
    wait(stage, es)
    wait(x_out, exs)
    wait(q_out, ezs)
    wait(q_in, ez)
    grad_ref[0] = (run + q_in[...].astype(f32)).T.astype(bf16)


def shards(features, layer_weight, cotangent, block_coords, block_counts, block_masks, edge_weight):
    vmem = pl.BlockSpec(memory_space=pltpu.VMEM)
    smem = pl.BlockSpec(memory_space=pltpu.SMEM)
    hbm = pl.BlockSpec(memory_space=pltpu.HBM)
    dma = pltpu.SemaphoreType.DMA
    ring = pltpu.VMEM((STEPS * NZ, B, FI), bf16)
    hops = dma((STEPS * NZ,))
    return pl.pallas_call(
        kernel,
        out_shape=(jax.ShapeDtypeStruct((1, B, FO), bf16), jax.ShapeDtypeStruct((1, B, FI), bf16)),
        in_specs=[smem] + [hbm] * 6,
        out_specs=(vmem, vmem),
        scratch_shapes=[
            pltpu.VMEM((N_ROW, B, FI), bf16), pltpu.VMEM((2, CAP), i32),
            pltpu.VMEM((CAP, B, B), i32), pltpu.VMEM((CAP, B, B), bf16), pltpu.VMEM((CAP, B, B), bf16),
            pltpu.VMEM((FI, FO), bf16), pltpu.VMEM((B, FO), bf16),
            pltpu.VMEM((8, 128), i32), pltpu.SMEM((8, 128), i32), pltpu.VMEM((CAP + 1, B, FI), f32),
            ring, ring, ring, ring,
            pltpu.VMEM((NZ - 1, B, FI), bf16), pltpu.VMEM((NZ, B, FI), bf16), pltpu.VMEM((N_COL, FI, B), bf16),
            pltpu.VMEM((ZH * NX, FI, B), f32), pltpu.VMEM((ZH * NX, FI, B), f32),
            pltpu.VMEM((6, FI, B), bf16), pltpu.VMEM((6, FI, B), bf16),
            pltpu.VMEM((FI, B), bf16), pltpu.VMEM((FI, B), bf16),
            dma((6,)), dma, dma((2, 3)), dma, dma((8,)),
            dma, hops, dma, hops, dma, dma((NZ,)),
            dma, hops, dma, hops, dma, dma((NZ,)),
            dma, dma((2,)), dma, dma((6,)), dma, dma,
        ],
        compiler_params=pltpu.CompilerParams(collective_id=0, has_side_effects=True, vmem_limit_bytes=VMEM_LIMIT),
    )(block_counts, jnp.swapaxes(block_coords, 2, 3), features, layer_weight, cotangent, block_masks, edge_weight)


def solution(mesh):
    return jax.shard_map(
        shards,
        mesh=mesh,
        in_specs=(
            P("col", "row", None),
            P(),
            P("row", "col", None),
            P("row", "col", None, None),
            P("row", "col"),
            P("row", "col", None, None, None),
            P("row", "col", None, None, None),
        ),
        out_specs=(P("row", "col", None), P("col", "row", None)),
        check_vma=False,
    )
```

time: 785 us -> 98.2 us (0.13)
  waiting for transfers between devices: 700 us -> 0 us
  Pallas kernels: 0 us -> 93.7 us
  blocking collectives: 47.1 us -> 0 us
  between operations: 14.5 us -> 1.29 us
  matrix products: 10.9 us -> 0 us
    reduce_scatter x2 -> x0, waiting for transfers between devices: 412 us -> none  [the longest x1 278 us: shards(): lax.psum_scatter(partial_value[None], 'col', scatter_dimension=1, tiled=T...]
    all_gather x1 -> x0, waiting for transfers between devices: 288 us -> none  [shards(): back_panel = lax.all_gather(back[None], 'col', axis=1, tiled=True)[0]]
    pallas_call x0 -> x1, Pallas kernels: none -> 93.7 us  [shards(): pl.pallas_call(kernel, out_shape=(jax.ShapeDtypeStruct((1, B, FO), bf16),...]
    all_gather x1 -> x0, blocking collectives: 47.1 us -> none  [shards(): panel = lax.all_gather(features, 'row', axis=1, tiled=True)[0]]
    dot_general x6 -> x0, matrix products: 10.9 us -> none  [the longest x2 4.95 us: block_sums(): jnp.einsum('kb,kif->bif', onehot, prod, precision=lax.Precision.HIGHEST)]
  transfers between devices with their start and end apart: 3 -> 0, of which waited for: 3 -> 0; matrix products, arithmetic and copies ran while one was open for 0% -> 0% of each run, Pallas kernels for 0% -> 0%
where the time goes in v2:
time: 98.2 us; the launch traced here: 98 us
  Pallas kernels  93.7 us (95%)
  local copies, waits for them, and re-layouts  2.94 us (3%)
  between operations  1.29 us (1%)
    pallas_call x1, Pallas kernels, shards(): pl.pallas_call(kernel, out_shape=(jax.ShapeDtypeStruct((1, B, FO), bf16),...  93.7 us
    unnamed x2, local copies, waits for them, and re-layouts  2.94 us

profile of v2, /device:TPU:1, one launch (start us, length us, event | category | flops | bytes accessed | tf_op | source)
XLA Modules:
  0.0 98.0 jit_solution(3173253699448612759)
XLA Ops:
  1.3 93.7 %shard_map.86 = (bf16[1,128,512]{2,1,0:T(8,128)(2,1)}, bf16[1,128,128]{2,1,0:T(8,128)(2,1)}) custom-call(s32[1,1]{1,0:T(1,128)S(6)} %copy.11.count_ref, s32[1,1,2,32]{3,2,1,0:T(2,128)} %bitcast.1, bf16[1,128,128]{2,1,0:T(8,128)(2,1)} %feat_hbm.1, bf16[128,512]{1,0:T(8,128)(2,1)} %w_hbm.1, bf16[1,128,512]{2,1,0:T(8,128)(2,1)} %cot_hbm.1, ...), custom_call_target="tpu_custom_call" | custom-call | tf_op jit(solution)/shard_map/pallas_call | solution.py:332
  95.0 1.6 %copy.12 = bf16[1,128,512]{2,1,0:T(8,128)(2,1)} copy(bf16[1,128,512]{2,1,0:T(8,128)(2,1)} %get-tuple-element.4) | data formatting | bytes 262144
  96.6 1.4 %copy.13 = bf16[1,128,128]{2,1,0:T(8,128)(2,1)} copy(bf16[1,128,128]{2,1,0:T(8,128)(2,1)} %get-tuple-element.5) | data formatting | bytes 65536

commit v3 on v2

--- a/solution.py
+++ b/solution.py
@@ -10,11 +10,12 @@
 NY, NZ = 8, 6
 N_ROW, N_COL = ZH * NX * NK, NY * NZ
 B = 128
-H = B // 2
 FI, FO = 128, 512
 CAP = 32
 STEPS = 4
-HALF = STEPS * NZ - NZ // 2
+HALF = 14
+FAR = 3
+WAVE = ((1, 0, 0), (1, 0, 1), (2, 3, 0), (2, 4, 0), (1, 0, 2), (2, 5, 0), (2, 3, 1), (1, 0, 3), (2, 4, 1), (2, 5, 1), (1, 0, 4))
 HIGHEST = lax.Precision.HIGHEST
 VMEM_LIMIT = 60 * 1024 * 1024
 f32, bf16, i32 = jnp.float32, jnp.bfloat16, jnp.int32
@@ -71,9 +72,9 @@
 
 def kernel(count_ref, coord_hbm, feat_hbm, w_hbm, cot_hbm, mask_hbm, weight_hbm, act_ref, grad_ref,
            panel, coord, mbuf, wbuf, blocks, wide, cot, table, tab, sums,
-           r_out, l_out, r_in, l_in, z_out, z_in, back,
+           r_out, l_out, r_in, l_in, n_out, n_in, z_out, z_in, acc, back,
            stage, c_in, x_out, x_in, q_out, q_in,
-           load, fs, fx, fz, fc, rs, rr, ls, lr, zs, zr, grs, grr, gls, glr, gzs, gzr, es, ec, exs, ex, ezs, ez):
+           load, fs, fx, fz, fc, rs, rr, ls, lr, ns, nr, zs, zr, grs, grr, gls, glr, gns, gnr, gzs, gzr, es, ec, exs, ex, ezs, ez):
     r = lax.axis_index("row")
     c = lax.axis_index("col")
     zh, x, k = r // (NX * NK), (r // NK) % NX, r % NK
@@ -84,9 +85,16 @@
     x_to = [(x + d) % NX for d in (1, 2, 3)]
     x_from = [(x + NX - d) % NX for d in (1, 2, 3)]
     x_peers = [(row_id(zh, t, k), c) for t in x_to]
-    right = (r, ((y + 1) % NY) * NZ + z)
-    left = (r, ((y + NY - 1) % NY) * NZ + z)
-    peers = [z_peer] + x_peers + [right, left] + [(r, y * NZ + (z + d) % NZ) for d in range(1, NZ)] + [c_peer]
+    ahead = [(r, ((y + d) % NY) * NZ + z) for d in (1, 2)]
+    behind = [(r, ((y + NY - d) % NY) * NZ + z) for d in (1, 2)]
+    side, m = 1 - 2 * (z // 3), jnp.minimum(z, NZ - 1 - z)
+    beside = [(z + 1, z < NZ - 1), (z - 1, z > 0), (z - 2 * side, m == 2)]
+    beyond = [(z + 2 * side, z >= 0), (z + 3 * side, z >= 0), (z + 4 * side, m <= 1), (z + 5 * side, m == 0)]
+
+    def line(column):
+        return (r, y * NZ + column)
+
+    peers = [z_peer] + x_peers + ahead + behind + [(r, y * NZ + (z + d) % NZ) for d in range(1, NZ)] + [c_peer]
     gate = pltpu.get_barrier_semaphore()
     for peer in peers:
         pl.semaphore_signal(gate, inc=1, device_id=peer, device_id_type=MESH)
@@ -158,76 +166,78 @@
 
     scan(0, lambda slot, source: jnp.dot(blocks[slot], panel[source], preferred_element_type=f32))
 
-    low, high = pl.ds(0, H), pl.ds(H, H)
-
-    def dest(j):
-        return near(z, NZ - 1 - j)
-
-    def part(dy, j):
-        return sums[tab[3, ((y + dy) % NY) * NZ + dest(j)]]
-
-    def first(j, carry):
-        mine = part(4, j).astype(bf16)
-        r_out[j, :H] = mine[:H]
-        send(r_out.at[j, low], r_in.at[j, low], rs, rr.at[j], right)
-        l_out[j, H:] = mine[H:]
-        send(l_out.at[j, high], l_in.at[j, high], ls, lr.at[j], left)
-        return carry
-
-    def second(j, carry):
-        t = NZ + j
-        mine = part(3, j)
-        wait(r_in.at[j, low], rr.at[j])
-        r_out[t, H:] = mine[H:].astype(bf16)
-        r_out[t, :H] = (mine[:H] + r_in[j, :H].astype(f32)).astype(bf16)
-        send(r_out.at[t], r_in.at[t], rs, rr.at[t], right)
-        mine = part(5, j)
-        wait(l_in.at[j, high], lr.at[j])
-        l_out[t, :H] = mine[:H].astype(bf16)
-        l_out[t, H:] = (mine[H:] + l_in[j, H:].astype(f32)).astype(bf16)
-        send(l_out.at[t], l_in.at[t], ls, lr.at[t], left)
-        return carry
-
-    def later(i, carry):
-        s, j = 2 + i // NZ, i % NZ
-        t = s * NZ + j
-        wait(r_in.at[t - NZ], rr.at[t - NZ])
-        r_out[t] = (part(STEPS - s, j) + r_in[t - NZ].astype(f32)).astype(bf16)
-        send(r_out.at[t], r_in.at[t], rs, rr.at[t], right)
-        wait(l_in.at[t - NZ], lr.at[t - NZ])
-        l_out[t] = (part(STEPS + s, j) + l_in[t - NZ].astype(f32)).astype(bf16)
-        send(l_out.at[t], l_in.at[t], ls, lr.at[t], left)
-        return carry
-
-    def collect(j):
-        t = 3 * NZ + j
-        wait(r_in.at[t], rr.at[t])
-        wait(l_in.at[t], lr.at[t])
-        return part(0, j) + r_in[t].astype(f32) + l_in[t].astype(f32)
-
-    def pass_on(j, carry):
-        z_out[j] = collect(j).astype(bf16)
-        send(z_out.at[j], z_in.at[z], zs, zr.at[z], (r, y * NZ + dest(j)))
-        return carry
-
-    lax.fori_loop(0, NZ, first, 0)
-    lax.fori_loop(0, NZ, second, 0)
-    lax.fori_loop(0, 2 * NZ, later, 0)
-    lax.fori_loop(0, NZ - 1, pass_on, 0)
+    def mine(dy, column):
+        return sums[tab[3, ((y + dy) % NY) * NZ + column]]
+
+    def joined(dy):
+        acc[...] = mine(dy, z)
+        for other, there in beside:
+
+            @pl.when(there)
+            def _():
+                q = other * NY + dy
+                wait(n_in.at[q], nr.at[q])
+                acc[...] = acc[...] + n_in[q].astype(f32)
+
+        return acc[...]
+
+    def ring(way):
+        return (r_out, r_in, rs, rr, ahead[0]) if way == 0 else (l_out, l_in, ls, lr, behind[0])
+
+    def hop(way, t, u):
+        out, arrive, out_sem, in_sem, peer = ring(way)
+        dy = STEPS - t if way == 0 else STEPS + t
+        run = joined(dy) if u == FAR else mine(dy, near(z, NZ - 1 - u))
+        p, q = (t - 1) * (FAR + 1) + u, t * (FAR + 1) + u
+        if t > (0 if way == u % 2 else 1):
+            wait(arrive.at[p], in_sem.at[p])
+            run = run + arrive[p].astype(f32)
+        out[q] = run.astype(bf16)
+        send(out.at[q], arrive.at[q], out_sem, in_sem.at[q], peer)
+
+    def stage_of(i, u):
+        hop(u % 2, i, u)
+        if i < STEPS - 1:
+            hop(1 - u % 2, i + 1, u)
+
+    def collect(u, run):
+        q = (STEPS - 1) * (FAR + 1) + u
+        wait(r_in.at[q], rr.at[q])
+        wait(l_in.at[q], lr.at[q])
+        return run + r_in[q].astype(f32) + l_in[q].astype(f32)
+
+    for u in range(FAR):
+        stage_of(0, u)
+    for n, dy in enumerate((4, 3, 5, 2, 6, 1, 7, 0)):
+        for i in (2, 1):
+            q = 2 * n + i - 1
+            n_out[q] = mine(dy, near(z, i)).astype(bf16)
+            send(n_out.at[q], n_in.at[z * NY + dy], ns, nr.at[z * NY + dy], line(near(z, i)))
+    for i in range(1, STEPS):
+        for u in range(FAR):
+            stage_of(i, u)
+        stage_of(i - 1, FAR)
+    for u in range(FAR):
+        z_out[u] = collect(u, mine(0, near(z, NZ - 1 - u))).astype(bf16)
+        send(z_out.at[u], z_in.at[z], zs, zr.at[z], line(near(z, NZ - 1 - u)))
+    stage_of(STEPS - 1, FAR)
 
     wait(panel.at[pl.ds(0, 15)], fs)
+    wait(n_out, ns)
     wait(r_out.at[pl.ds(0, HALF)], rs)
     wait(l_out.at[pl.ds(0, HALF)], ls)
     local[4].wait()
     local[5].wait()
     weight = wide[...].astype(f32)
-
-    def take(i, run):
-        other = near(z, i)
-        wait(z_in.at[other], zr.at[other])
-        return run + z_in[other].astype(f32)
-
-    total = lax.fori_loop(1, NZ, take, collect(NZ - 1))
+    acc[...] = collect(FAR, joined(0))
+    for other, there in beyond:
+
+        @pl.when(there)
+        def _():
+            wait(z_in.at[other], zr.at[other])
+            acc[...] = acc[...] + z_in[other].astype(f32)
+
+    total = acc[...]
 
     pre = jnp.dot(total, weight, precision=HIGHEST, preferred_element_type=f32)
     scale = 0.7978845608028654
@@ -241,52 +251,66 @@
     def block(dy, j):
         return back.at[((y + dy) % NY) * NZ + near(z, j)]
 
-    def hop(s, j):
-        t = s * NZ + j
-        if s < STEPS - 1:
-            right_ref, left_ref = block(NY - s, j), block(s, j)
-        else:
-            right_ref, left_ref = block(NY - s, j).at[low], block(s, j).at[high]
-        send(right_ref, right_ref, grs, grr.at[t], right)
-        send(left_ref, left_ref, gls, glr.at[t], left)
-
-    mine = back.at[c]
-    for j in range(1, NZ):
-        send(mine, mine, gzs, gzr.at[z], (r, y * NZ + near(z, NZ - j)))
-    act_ref[0] = (pre * cdf).astype(bf16)
-
-    def wave(i, carry):
-        for s in range(STEPS - 1, 0, -1):
-            j = i - 3 * s
-
-            @pl.when((j >= 0) & (j < NZ))
+    def forward(way, d, tag, j):
+        ref = block(NY - (tag - d), j) if way == 0 else block(tag - d, j)
+        sems = (grs, grr) if way == 0 else (gls, glr)
+        send(ref, ref, sems[0], sems[1].at[(tag - 1) * NZ + j], (ahead if way == 0 else behind)[d - 1])
+
+    def arrived(way, tag, j):
+        wait(block(NY - tag, j) if way == 0 else block(tag, j), (grr if way == 0 else glr).at[(tag - 1) * NZ + j])
+
+    def share(dy):
+        at = ((y + dy) % NY) * NZ + z
+        for i, (other, there) in enumerate(beside):
+
+            @pl.when(there)
             def _():
-                t = (s - 1) * NZ + j
-                wait(block(NY - s, j), grr.at[t])
-                wait(block(s, j), glr.at[t])
-                hop(s, j)
-
-        @pl.when((i > 0) & (i < NZ))
-        def _():
-            other = near(z, i)
+                send(back.at[at], back.at[at], gns.at[i], gnr.at[at], line(other))
+
+    for step, j, s in WAVE:
+        long_way = j % 2
+        if s == 0 and j > 0:
+            other = near(z, j)
             wait(back.at[y * NZ + other], gzr.at[other])
-
-        @pl.when(i < NZ)
-        def _():
-            hop(0, i)
-
-        return carry
-
-    lax.fori_loop(0, NZ + 3 * (STEPS - 1), wave, 0)
+        for way in (long_way, 1 - long_way):
+            reach = STEPS if way == long_way else STEPS - 1
+            if step == 1:
+                if 0 < s <= reach:
+                    arrived(way, s, j)
+                if s < reach:
+                    forward(way, 1, s + 1, j)
+            elif s == 0:
+                forward(way, 2, 2, j)
+                forward(way, 1, 1, j)
+            else:
+                arrived(way, 2, j)
+                if reach == STEPS:
+                    forward(way, 2, 4, j)
+                forward(way, 1, 3, j)
+        if j == 0:
+            if s == 0:
+                for i in (3, 2, 1, 0):
+                    other, there = beyond[i]
+
+                    @pl.when(there)
+                    def _():
+                        send(back.at[c], back.at[c], gzs.at[i], gzr.at[z], line(other))
+
+            share(NY - s)
+            if 0 < s < STEPS:
+                share(s)
+            if s == 0:
+                act_ref[0] = (pre * cdf).astype(bf16)
     wait(z_out, zs)
-
-    def finish(j, carry):
-        t = (STEPS - 1) * NZ + j
-        wait(block(STEPS, j).at[low], grr.at[t])
-        wait(block(STEPS, j).at[high], glr.at[t])
-        return carry
-
-    lax.fori_loop(0, NZ, finish, 0)
+    for j in range(FAR, NZ):
+        for way in (j % 2, 1 - j % 2):
+            arrived(way, 1, j)
+            arrived(way, 3, j)
+        arrived(j % 2, 4, j)
+    for i in (1, 2):
+        for t in range(NY):
+            at = t * NZ + near(z, i)
+            wait(back.at[at], gnr.at[at])
 
     scan(4, lambda slot, source: jnp.dot(back[source], blocks[slot], preferred_element_type=f32))
 
@@ -314,7 +338,18 @@
             send(q_out, q_in, ezs, ez, z_peer)
     wait(back.at[pl.ds(0, HALF)], grs)
     wait(back.at[pl.ds(0, HALF)], gls)
-    wait(z_out, gzs)
+    for i, (other, there) in enumerate(beside):
+
+        @pl.when(there)
+        def _():
+            wait(back.at[pl.ds(0, NY)], gns.at[i])
+
+    for i, (other, there) in enumerate(beyond):
+
+        @pl.when(there)
+        def _():
+            wait(back.at[0], gzs.at[i])
+
     wait(stage, es)
     wait(x_out, exs)
     wait(q_out, ezs)
@@ -327,8 +362,9 @@
     smem = pl.BlockSpec(memory_space=pltpu.SMEM)
     hbm = pl.BlockSpec(memory_space=pltpu.HBM)
     dma = pltpu.SemaphoreType.DMA
-    ring = pltpu.VMEM((STEPS * NZ, B, FI), bf16)
-    hops = dma((STEPS * NZ,))
+    ring = pltpu.VMEM((STEPS * (FAR + 1), B, FI), bf16)
+    hop = dma((STEPS * (FAR + 1),))
+    hop_back = dma((STEPS * NZ,))
     return pl.pallas_call(
         kernel,
         out_shape=(jax.ShapeDtypeStruct((1, B, FO), bf16), jax.ShapeDtypeStruct((1, B, FI), bf16)),
@@ -340,13 +376,14 @@
             pltpu.VMEM((FI, FO), bf16), pltpu.VMEM((B, FO), bf16),
             pltpu.VMEM((8, 128), i32), pltpu.SMEM((8, 128), i32), pltpu.VMEM((CAP + 1, B, FI), f32),
             ring, ring, ring, ring,
-            pltpu.VMEM((NZ - 1, B, FI), bf16), pltpu.VMEM((NZ, B, FI), bf16), pltpu.VMEM((N_COL, FI, B), bf16),
+            pltpu.VMEM((2 * NY, B, FI), bf16), pltpu.VMEM((N_COL, B, FI), bf16), pltpu.VMEM((FAR, B, FI), bf16),
+            pltpu.VMEM((NZ, B, FI), bf16), pltpu.VMEM((B, FI), f32), pltpu.VMEM((N_COL, FI, B), bf16),
             pltpu.VMEM((ZH * NX, FI, B), f32), pltpu.VMEM((ZH * NX, FI, B), f32),
             pltpu.VMEM((6, FI, B), bf16), pltpu.VMEM((6, FI, B), bf16),
             pltpu.VMEM((FI, B), bf16), pltpu.VMEM((FI, B), bf16),
             dma((6,)), dma, dma((2, 3)), dma, dma((8,)),
-            dma, hops, dma, hops, dma, dma((NZ,)),
-            dma, hops, dma, hops, dma, dma((NZ,)),
+            dma, hop, dma, hop, dma, dma((N_COL,)), dma, dma((NZ,)),
+            dma, hop_back, dma, hop_back, dma((3,)), dma((N_COL,)), dma((4,)), dma((NZ,)),
             dma, dma((2,)), dma, dma((6,)), dma, dma,
         ],
         compiler_params=pltpu.CompilerParams(collective_id=0, has_side_effects=True, vmem_limit_bytes=VMEM_LIMIT),

time: 98.2 us -> 93.9 us (0.956)
  Pallas kernels: 93.7 us -> 89.5 us
    pallas_call x1, Pallas kernels: 93.7 us -> 89.5 us  [shards(): pl.pallas_call(kernel, out_shape=(jax.ShapeDtypeStruct((1, B, FO), bf16),...]
where the time goes in v3:
time: 93.9 us; the launch traced here: 93.7 us
  Pallas kernels  89.5 us (95%)
  local copies, waits for them, and re-layouts  2.94 us (3%)
  between operations  1.29 us (1%)
    pallas_call x1, Pallas kernels, shards(): pl.pallas_call(kernel, out_shape=(jax.ShapeDtypeStruct((1, B, FO), bf16),...  89.5 us
    unnamed x2, local copies, waits for them, and re-layouts  2.94 us

profile of v3, /device:TPU:1, one launch (start us, length us, event | category | flops | bytes accessed | tf_op | source)
XLA Modules:
  0.0 93.7 jit_solution(13983321318656781586)
XLA Ops:
  1.3 89.5 %shard_map.86 = (bf16[1,128,512]{2,1,0:T(8,128)(2,1)}, bf16[1,128,128]{2,1,0:T(8,128)(2,1)}) custom-call(s32[1,1]{1,0:T(1,128)S(6)} %copy.11.count_ref, s32[1,1,2,32]{3,2,1,0:T(2,128)} %bitcast.1, bf16[1,128,128]{2,1,0:T(8,128)(2,1)} %feat_hbm.1, bf16[128,512]{1,0:T(8,128)(2,1)} %w_hbm.1, bf16[1,128,512]{2,1,0:T(8,128)(2,1)} %cot_hbm.1, ...), custom_call_target="tpu_custom_call" | custom-call | tf_op jit(solution)/shard_map/pallas_call | solution.py:368
  90.8 1.6 %copy.12 = bf16[1,128,512]{2,1,0:T(8,128)(2,1)} copy(bf16[1,128,512]{2,1,0:T(8,128)(2,1)} %get-tuple-element.4) | data formatting | bytes 262144
  92.3 1.4 %copy.13 = bf16[1,128,128]{2,1,0:T(8,128)(2,1)} copy(bf16[1,128,128]{2,1,0:T(8,128)(2,1)} %get-tuple-element.5) | data formatting | bytes 65536

commit v4 on v3

--- a/solution.py
+++ b/solution.py
@@ -17,7 +17,7 @@
 FAR = 3
 WAVE = ((1, 0, 0), (1, 0, 1), (2, 3, 0), (2, 4, 0), (1, 0, 2), (2, 5, 0), (2, 3, 1), (1, 0, 3), (2, 4, 1), (2, 5, 1), (1, 0, 4))
 HIGHEST = lax.Precision.HIGHEST
-VMEM_LIMIT = 60 * 1024 * 1024
+VMEM_LIMIT = 537 * 1024 * 1024 // 10
 f32, bf16, i32 = jnp.float32, jnp.bfloat16, jnp.int32
 
 
@@ -320,16 +320,16 @@
     halves = (1 - zh, zh)
     for i, h in enumerate(halves):
         for t in range(NX):
-            stage[h * NX + t] = grad(h, t, 1 - k)
+            stage[h * NX + t] = grad(h, t, 1 - k).astype(bf16)
         at = pl.ds(h * NX, NX)
         send(stage.at[at], c_in.at[at], es, ec.at[i], c_peer)
     for i, h in enumerate(halves):
         wait(c_in.at[pl.ds(h * NX, NX)], ec.at[i])
         for d in (1, 0, 2):
-            x_out[i * 3 + d] = (grad(h, x_to[d], k) + c_in[h * NX + x_to[d]]).astype(bf16)
+            x_out[i * 3 + d] = (grad(h, x_to[d], k) + c_in[h * NX + x_to[d]].astype(f32)).astype(bf16)
             send(x_out.at[i * 3 + d], x_in.at[i * 3 + d], exs, ex.at[i * 3 + d], x_peers[d])
     for i, h in enumerate(halves):
-        run = grad(h, x, k) + c_in[h * NX + x]
+        run = grad(h, x, k) + c_in[h * NX + x].astype(f32)
         for d in (0, 2, 1):
             wait(x_in.at[i * 3 + d], ex.at[i * 3 + d])
             run = run + x_in[i * 3 + d].astype(f32)
@@ -378,7 +378,7 @@
             ring, ring, ring, ring,
             pltpu.VMEM((2 * NY, B, FI), bf16), pltpu.VMEM((N_COL, B, FI), bf16), pltpu.VMEM((FAR, B, FI), bf16),
             pltpu.VMEM((NZ, B, FI), bf16), pltpu.VMEM((B, FI), f32), pltpu.VMEM((N_COL, FI, B), bf16),
-            pltpu.VMEM((ZH * NX, FI, B), f32), pltpu.VMEM((ZH * NX, FI, B), f32),
+            pltpu.VMEM((ZH * NX, FI, B), bf16), pltpu.VMEM((ZH * NX, FI, B), bf16),
             pltpu.VMEM((6, FI, B), bf16), pltpu.VMEM((6, FI, B), bf16),
             pltpu.VMEM((FI, B), bf16), pltpu.VMEM((FI, B), bf16),
             dma((6,)), dma, dma((2, 3)), dma, dma((8,)),

time: 93.9 us -> 93.2 us (level)
    unnamed x2 -> x6, local copies, waits for them, and re-layouts: 2.94 us -> 2.7 us
where the time goes in v4:
time: 93.2 us; the launch traced here: 93 us
  Pallas kernels  89 us (95%)
  local copies, waits for them, and re-layouts  2.7 us (3%)
  between operations  1.3 us (1%)
    pallas_call x1, Pallas kernels, shards(): pl.pallas_call(kernel, out_shape=(jax.ShapeDtypeStruct((1, B, FO), bf16),...  89 us
    unnamed x6, local copies, waits for them, and re-layouts  2.7 us

profile of v4, /device:TPU:1, one launch (start us, length us, event | category | flops | bytes accessed | tf_op | source)
XLA Modules:
  0.0 93.0 jit_solution(7935922600872940504)
XLA Ops:
  1.3 0.0 copy-start
  1.3 0.7 copy-done
  2.0 0.0 copy-start.1
  2.0 0.7 copy-done.1
  2.7 89.0 %shard_map.86 = (bf16[1,128,512]{2,1,0:T(8,128)(2,1)S(1)}, bf16[1,128,128]{2,1,0:T(8,128)(2,1)S(1)}) custom-call(s32[1,1]{1,0:T(1,128)S(6)} %copy.11.count_ref, s32[1,1,2,32]{3,2,1,0:T(2,128)S(1)} %bitcast.1, bf16[1,128,128]{2,1,0:T(8,128)(2,1)S(1)} %copy-done, bf16[128,512]{1,0:T(8,128)(2,1)} %w_hbm.1, bf16[1,128,512]{2,1,0:T(8,128)(2,1)} %cot_hbm.1, ...), custom_call_target="tpu_custom_call" | custom-call | tf_op jit(solution)/shard_map/pallas_call | solution.py:368
  91.7 0.7 copy.12
  92.3 0.6 copy.13
Async XLA Ops:
  1.3 0.8 copy-start
  2.0 0.7 copy-start.1
